TPU v7x, 128 devices: a whole 4x4x4 slice. The times are simulated.
128 devices in a mesh: depth: 32 (over z, x, core), tile: 4 (over y).
Axes of the slice: x: 4, y: 4, z: 4, core: 2. Of those that a mesh axis runs over, the one named last changes fastest.
Arguments:
- field: float32 [64, 512, 2048], P('depth', None, 'tile'), may hold values from -6 to 6
- bin_ids: int32 [64, 512, 2048], P('depth', None, 'tile'), may hold values from 0 to 255
- table_color: bfloat16 [3, 256], replicated, may hold values from 0.02 to 1
- table_opacity: bfloat16 [256], replicated, may hold values from 0.015 to 0.15
Outputs:
- front_image: float32 [4, 512, 2048], P(None, 'depth', 'tile')
- back_image: float32 [4, 512, 2048], P(None, 'depth', 'tile')
All inputs are finite; a program needn't handle non-finite values.
Results may differ from a plain program's by a relative error of at most 0.0003.
Values sent between devices are 32-bit elements; how exact they have to be, the bound alone decides.
A program may use at most 128 MiB of HBM per device.

v0:
```python
import jax
import jax.numpy as jnp
from jax import lax
from jax.experimental import pallas as pl
from jax.experimental.pallas import tpu as pltpu
from jax.sharding import PartitionSpec as P

MESH = pl.DeviceIdType.MESH
F32 = jnp.float32
NZ, NX, NC = 4, 4, 2
NR = NX * NC
NS = 2 * NR
BR = 16
NT = 4
TOP = 8
HALF = NZ * NT


def kernel(
    field, bins, tcol_h, topa_h, front, back,
    tcol, topa, fb, bb, hb, hs, fv, ga, gl, stage, img,
    lsem, fsem, bsem, hsem, zsem, ysem, csem, isem, sx, sh, sz, sy, sc, si,
):
    d = lax.axis_index("depth")
    y = lax.axis_index("tile")
    ny = lax.axis_size("tile")
    z = d // NR
    xc = d % NR
    x = xc // NC
    c = xc % NC

    load = pltpu.make_async_copy(field, fv, lsem.at[0])
    load.start()
    tload = [pltpu.make_async_copy(tcol_h, tcol, lsem.at[1]), pltpu.make_async_copy(topa_h, topa, lsem.at[2])]
    for cp in tload:
        cp.start()
    bar = pltpu.get_barrier_semaphore()
    for p in range(1, NR):
        pl.semaphore_signal(bar, inc=1, device_id=(z * NR + (xc + p) % NR, y), device_id_type=MESH)
    for p in range(1, NZ):
        pl.semaphore_signal(bar, inc=1, device_id=((z + p) % NZ * NR + xc, y), device_id_type=MESH)
    for p in (1, ny - 1):
        pl.semaphore_signal(bar, inc=1, device_id=(d, (y + p) % ny), device_id_type=MESH)

    @pl.when(y == 0)
    def _():
        fb[:, 0, 2:2 + NS, TOP:TOP + BR, :] = jnp.zeros((NZ, NS, BR, 128), F32)

    @pl.when(y == ny - 1)
    def _():
        fb[:, NT + 1, 2:2 + NS, TOP:TOP + BR, :] = jnp.zeros((NZ, NS, BR, 128), F32)

    @pl.when(z == 0)
    def _():
        fb[:, 1:NT + 1, 0:2, TOP:TOP + BR, :] = jnp.zeros((NZ, NT, 2, BR, 128), F32)

    @pl.when(z == NZ - 1)
    def _():
        fb[:, 1:NT + 1, NS + 2:NS + 4, TOP:TOP + BR, :] = jnp.zeros((NZ, NT, 2, BR, 128), F32)

    pl.semaphore_wait(bar, NR - 1 + NZ - 1 + 2)

    def rows_of(zb, q):
        return pl.ds(pl.multiple_of((zb * NX + q // NC) * BR * NC + q % NC * BR, BR), BR)

    def copy_x(src, dst, send, recv, q):
        return pltpu.make_async_remote_copy(
            src_ref=src, dst_ref=dst, send_sem=send, recv_sem=recv,
            device_id=(z * NR + q, y), device_id_type=MESH)

    def bin_tile(m):
        t = m // NT
        mixed = (t % 3 + 1) // 2
        off = mixed * (1 + 2 * (m % 2)) + (1 - mixed) * 2 * (1 - t // 3)
        return (z + off) % NZ, mixed * ((m - NT) // 2) + (1 - mixed) * (m % NT)

    def tick_refs(n, q):
        f_zb, f_j = n // NT, n % NT
        b_zb, b_j = bin_tile(n - HALF)
        f_cols = pl.ds(pl.multiple_of(128 * f_j, 128), 128)
        b_cols = pl.ds(pl.multiple_of(128 * b_j, 128), 128)
        return (
            (field.at[:, rows_of(f_zb, q), f_cols], fb.at[f_zb, f_j + 1, pl.ds(2 + 2 * xc, 2), pl.ds(TOP, BR), :]),
            (bins.at[:, rows_of(b_zb, q), b_cols], bb.at[b_zb, pl.ds(2 * xc, 2), :, b_cols]),
        )

    def send_tick(n, k=0):
        for kind in range(2):
            @pl.when(n // HALF == kind)
            def _():
                recv = bsem.at[n - HALF] if kind else fsem.at[n // NT]
                src, dst = tick_refs(n, xc)[kind]
                pltpu.make_async_copy(src, dst, recv).start()

                def one(p, k2):
                    q = (xc + p) % NR
                    src, dst = tick_refs(n, q)[kind]
                    copy_x(src, dst, sx.at[n], recv, q).start()
                    return k2

                lax.fori_loop(1, NR, one, 0)
        return k

    def tick_left(n):
        some = bb.at[0, pl.ds(0, NS - 2), :, pl.ds(0, 128)]
        pltpu.make_async_copy(some, some, sx.at[n]).wait()

    def send_h():
        pltpu.make_async_copy(hs.at[xc], hb.at[xc], hsem.at[0]).start()

        def one(p, k):
            q = (xc + p) % NR
            copy_x(hs.at[q], hb.at[xc], sh.at[0], hsem.at[0], q).start()
            return k

        lax.fori_loop(1, NR, one, 0)

    lax.fori_loop(0, NT, send_tick, 0)

    load.wait()
    total = NZ * NX * NC * BR
    for q in range(NR):
        for zb in range(NZ):
            r0 = (zb * NX + q // NC) * BR * NC + (BR * NC if q % NC else -2)
            for s in range(2):
                o = zb % 2 * 4 + s * 2
                for j in range(NT):
                    if 0 <= r0 < total:
                        hs[q, zb // 2, j, o:o + 2, :] = fv[s, r0:r0 + 2, 128 * j:128 * j + 128]
                    else:
                        hs[q, zb // 2, j, o:o + 2, :] = jnp.zeros((2, 128), F32)

    send_h()
    lax.fori_loop(NT, 2 * HALF, send_tick, 0)

    for cp in tload:
        cp.wait()
    tc = tcol[...].astype(F32)
    to_ = topa[...].astype(F32).reshape(1, -1) * (1.0 / 144.0)
    tabs = []
    for k in range(3):
        tabs.append([jnp.broadcast_to(tc[k:k + 1, 128 * h:128 * h + 128], (8, 128)) for h in range(2)])
    tabs.append([jnp.broadcast_to(to_[:, 128 * h:128 * h + 128], (8, 128)) for h in range(2)])

    def z_copy(zb, up):
        src = fb.at[zb, pl.ds(1, NT), pl.ds(NS if up else 2, 2), pl.ds(TOP, BR), :]
        dst = fb.at[zb, pl.ds(1, NT), pl.ds(0 if up else NS + 2, 2), pl.ds(TOP, BR), :]
        return pltpu.make_async_remote_copy(
            src_ref=src, dst_ref=dst, send_sem=sz.at[zb, int(up)], recv_sem=zsem.at[zb, int(up)],
            device_id=(d + (NR if up else -NR), y), device_id_type=MESH)

    def y_copy(zb, right):
        src = fb.at[zb, NT if right else 1, pl.ds(2, NS), pl.ds(TOP, BR), :]
        dst = fb.at[zb, 0 if right else NT + 1, pl.ds(2, NS), pl.ds(TOP, BR), :]
        return pltpu.make_async_remote_copy(
            src_ref=src, dst_ref=dst, send_sem=sy.at[zb, int(right)], recv_sem=ysem.at[zb, int(right)],
            device_id=(d, y + (1 if right else -1)), device_id_type=MESH)

    def c_copy(zb):
        src = fb.at[zb, pl.ds(1, NT), pl.ds(2, NS), pl.ds(pl.multiple_of(TOP + 8 * (1 - c), 8), 8), :]
        dst = fb.at[zb, pl.ds(1, NT), pl.ds(2, NS), pl.ds(pl.multiple_of((TOP + BR) * c, 8), 8), :]
        return pltpu.make_async_remote_copy(
            src_ref=src, dst_ref=dst, send_sem=sc.at[zb], recv_sem=csem.at[zb],
            device_id=(d + 1 - 2 * c, y), device_id_type=MESH)

    def pass_on(zb):
        own = fb.at[zb, pl.ds(1, NT), pl.ds(2, NS), pl.ds(TOP, BR), :]
        pltpu.make_async_copy(own, own, fsem.at[zb]).wait()

        @pl.when(z < NZ - 1)
        def _():
            z_copy(zb, True).start()

        @pl.when(z > 0)
        def _():
            z_copy(zb, False).start()

        @pl.when(y > 0)
        def _():
            y_copy(zb, False).start()

        @pl.when(y < ny - 1)
        def _():
            y_copy(zb, True).start()

        c_copy(zb).start()

    def rows_in(i, k, at):
        for zb in range(NZ):
            for s in range(2):
                a = zb % 2 * 4 + s * 2
                for j in range(NT):
                    fb[zb, j + 1, 2 + 2 * i + s, at:at + 2, :] = hb[i, zb // 2, j, a:a + 2, :]
        return k

    def all_rows_in():
        pltpu.make_async_copy(hb, hb, hsem.at[0]).wait()

        @pl.when(c == 0)
        def _():
            lax.fori_loop(0, NR, lambda i, k: rows_in(i, k, TOP - 2), 0)

        @pl.when(c == 1)
        def _():
            lax.fori_loop(0, NR, lambda i, k: rows_in(i, k, TOP + BR), 0)

    def halos(zb):
        @pl.when(z > 0)
        def _():
            z_copy(zb, True).wait_recv()

        @pl.when(z < NZ - 1)
        def _():
            z_copy(zb, False).wait_recv()

        @pl.when(y > 0)
        def _():
            y_copy(zb, True).wait_recv()

        @pl.when(y < ny - 1)
        def _():
            y_copy(zb, False).wait_recv()

        c_copy(zb).wait_recv()

    lane = lax.broadcasted_iota(jnp.int32, (8, 128), 1)
    kd, kr, kc = 0.7 * 0.48 / 12.0, 0.7 * 0.6 / 12.0, 0.7 * 0.64 / 12.0

    def gradients(zb, j, g):
        r = pl.multiple_of(TOP + 8 * g, 8)
        rows = pl.ds(pl.multiple_of(8 * g, 8), 8)
        lanes = pl.ds(pl.multiple_of(128 * j, 128), 128)
        win = [fb[zb, j + 1, s, pl.ds(r, 8), :] for s in range(4)]
        for s in range(NS):
            win.append(fb[zb, j + 1, s + 4, pl.ds(r, 8), :])
            v = win[s + 2]
            gd = 8.0 * (win[s + 3] - win[s + 1]) + (win[s] - win[s + 4])
            m2, m1, p1, p2 = [fb[zb, j + 1, s + 2, pl.ds(r + o, 8), :] for o in (-2, -1, 1, 2)]
            gr = 8.0 * (p1 - m1) + (m2 - p2)
            lt = fb[zb, j, s + 2, pl.ds(r, 8), :]
            rt = fb[zb, j + 2, s + 2, pl.ds(r, 8), :]
            l1 = pltpu.roll(jnp.where(lane == 127, lt, v), 1, 1)
            l2 = pltpu.roll(jnp.where(lane >= 126, lt, v), 2, 1)
            r1 = pltpu.roll(jnp.where(lane == 0, rt, v), 127, 1)
            r2 = pltpu.roll(jnp.where(lane < 2, rt, v), 126, 1)
            gc = 8.0 * (r1 - l1) + (l2 - r2)
            q = gd * gd + gr * gr + gc * gc
            inv = lax.rsqrt(q * (1.0 / 144.0) + 1.0)
            a = q * (inv * inv)
            ga[zb, s, rows, lanes] = a
            gl[zb, s, rows, lanes] = a * (0.3 + jnp.abs(kd * gd + kr * gr + kc * gc) * inv)

    def shade(zb, j, g, m):
        rows = pl.ds(pl.multiple_of(8 * g, 8), 8)
        lanes = pl.ds(pl.multiple_of(128 * j, 128), 128)
        fr = [jnp.zeros((8, 128), F32) for _ in range(3)]
        bk = [jnp.zeros((8, 128), F32) for _ in range(3)]
        tr = jnp.ones((8, 128), F32)
        for s in range(NS):
            ids = bb[zb, s, rows, lanes]
            low = ids & 127
            upper = ids >= 128
            look = [
                jnp.where(upper,
                          jnp.take_along_axis(hi, low, axis=1, mode="promise_in_bounds"),
                          jnp.take_along_axis(lo, low, axis=1, mode="promise_in_bounds"))
                for lo, hi in tabs
            ]
            keep = 1.0 - look[3] * ga[zb, s, rows, lanes]
            w = look[3] * gl[zb, s, rows, lanes]
            for k in range(3):
                col = look[k] * w
                fr[k] = fr[k] + tr * col
                bk[k] = bk[k] * keep + col
            tr = tr * keep
        for k, part in enumerate(fr + bk + [tr]):
            stage[m, k, rows, :] = part

    def i_copy(m):
        zb, j = bin_tile(m)
        return pltpu.make_async_remote_copy(
            src_ref=stage.at[m], dst_ref=img.at[z, j], send_sem=si.at[m], recv_sem=isem.at[z, j],
            device_id=(zb * NR + xc, y), device_id_type=MESH)

    def finish(m):
        j = m % NT
        img[z, j] = stage[m]
        for p in range(1, NZ):
            other = img.at[(z + p) % NZ, j]
            pltpu.make_async_copy(other, other, isem.at[(z + p) % NZ, j]).wait()
        lanes = pl.ds(pl.multiple_of(128 * j, 128), 128)
        ts = [img[s, j, 6] for s in range(NZ)]
        t = (ts[0] * ts[1]) * (ts[2] * ts[3])
        for n in range(3):
            acc = img[NZ - 1, j, n]
            for s in range(NZ - 2, -1, -1):
                acc = img[s, j, n] + ts[s] * acc
            front[n, :, lanes] = acc
            acc = img[0, j, 3 + n]
            for s in range(1, NZ):
                acc = img[s, j, 3 + n] + ts[s] * acc
            back[n, :, lanes] = acc
        front[3, :, lanes] = t
        back[3, :, lanes] = t

    def cells_in(n, k):
        pl.when(n < NZ)(lambda: pass_on(n))
        pl.when(n == 1)(all_rows_in)

        @pl.when(n > 0)
        def _():
            halos(n - 1)

            def part(h, k2):
                gradients(n - 1, h // 2, h % 2)
                return k2

            lax.fori_loop(0, 2 * NT, part, 0)
        return k

    lax.fori_loop(0, NZ + 1, cells_in, 0)

    def bins_in(m, k):
        zb, j = bin_tile(m)
        got = bb.at[zb, :, :, pl.ds(pl.multiple_of(128 * j, 128), 128)]
        pltpu.make_async_copy(got, got, bsem.at[m]).wait()

        def part(h, k2):
            shade(zb, j, h, m)
            return k2

        lax.fori_loop(0, 2, part, 0)
        pl.when(m < HALF - NT)(lambda: i_copy(m).start())
        pl.when(m >= HALF - NT)(lambda: finish(m))
        return k

    lax.fori_loop(0, HALF, bins_in, 0)

    def ticks(n, k):
        tick_left(n)
        return k

    lax.fori_loop(0, 2 * HALF, ticks, 0)
    def left(zb, k):
        @pl.when(z < NZ - 1)
        def _():
            z_copy(zb, True).wait_send()

        @pl.when(z > 0)
        def _():
            z_copy(zb, False).wait_send()

        @pl.when(y > 0)
        def _():
            y_copy(zb, False).wait_send()

        @pl.when(y < ny - 1)
        def _():
            y_copy(zb, True).wait_send()

        c_copy(zb).wait_send()
        return k

    lax.fori_loop(0, NZ, left, 0)
    some = hb.at[pl.ds(0, NR - 1)]
    pltpu.make_async_copy(some, some, sh.at[0]).wait()

    def shown(m, k):
        i_copy(m).wait_send()
        return k

    lax.fori_loop(0, HALF - NT, shown, 0)


def local(field, bin_ids, table_color, table_opacity):
    cols = field.shape[2]
    out = jax.ShapeDtypeStruct((4, BR, cols), F32)
    vm = pl.BlockSpec(memory_space=pltpu.VMEM)
    hbm = pl.BlockSpec(memory_space=pltpu.HBM)
    dma = pltpu.SemaphoreType.DMA
    args = [
        pltpu.with_memory_space_constraint(a, pltpu.HBM)
        for a in (field, bin_ids, table_color, table_opacity)
    ]
    return pl.pallas_call(
        kernel,
        out_shape=(out, out),
        in_specs=[hbm] * 4,
        out_specs=(vm, vm),
        scratch_shapes=[
            pltpu.VMEM(table_color.shape, table_color.dtype),
            pltpu.VMEM(table_opacity.shape, table_opacity.dtype),
            pltpu.VMEM((NZ, NT + 2, NS + 4, BR + 16, 128), F32),
            pltpu.VMEM((NZ, NS, BR, cols), jnp.int32),
            pltpu.VMEM((NR, 2, NT, 8, 128), F32),
            pltpu.VMEM((NR, 2, NT, 8, 128), F32),
            pltpu.VMEM(field.shape, F32),
            pltpu.VMEM((NZ, NS, BR, cols), F32),
            pltpu.VMEM((NZ, NS, BR, cols), F32),
            pltpu.VMEM((HALF, 7, BR, 128), F32),
            pltpu.VMEM((NZ, NT, 7, BR, 128), F32),
            dma((3,)), dma((NZ,)), dma((HALF,)), dma((1,)), dma((NZ, 2)), dma((NZ, 2)), dma((NZ,)), dma((NZ, NT)),
            dma((2 * HALF,)), dma((1,)), dma((NZ, 2)), dma((NZ, 2)), dma((NZ,)), dma((HALF,)),
        ],
        compiler_params=pltpu.CompilerParams(
            collective_id=0, has_side_effects=True, vmem_limit_bytes=40 * 2**20),
    )(*args)


def solution(mesh):
    return jax.shard_map(
        local,
        mesh=mesh,
        in_specs=(P("depth", None, "tile"), P("depth", None, "tile"), P(), P()),
        out_specs=(P(None, "depth", "tile"), P(None, "depth", "tile")),
        check_vma=False,
    )
```

profile of v0, /device:TPU:1, one launch (start us, length us, event | category | flops | bytes accessed | tf_op | source)
XLA Modules:
  0.0 60.6 jit_solution(16469199041518061669)
XLA Ops:
  0.6 58.6 %shard_map.59 = (f32[4,16,512]{2,1,0:T(8,128)S(1)}, f32[4,16,512]{2,1,0:T(8,128)S(1)}) custom-call(f32[2,512,512]{2,1,0:T(8,128)} %field.1, s32[2,512,512]{2,1,0:T(8,128)} %bins.1, bf16[3,256]{1,0:T(4,128)(2,1)} %tcol_h.1, bf16[256]{0:T(256)(128)(2,1)} %topa_h.1), custom_call_target="tpu_custom_call" | custom-call | tf_op jit(solution)/shard_map/pallas_call | solution.py:385
  59.2 0.7 %copy.8 = f32[4,16,512]{2,1,0:T(8,128)} copy(f32[4,16,512]{2,1,0:T(8,128)S(1)} %get-tuple-element.4) | data formatting | bytes 262144
  59.9 0.7 %copy.9 = f32[4,16,512]{2,1,0:T(8,128)} copy(f32[4,16,512]{2,1,0:T(8,128)S(1)} %get-tuple-element.5) | data formatting | bytes 262144
where the time goes:
time: 60.7 us; the launch traced here: 60.6 us
  Pallas kernels  58.6 us (97%)
  local copies, waits for them, and re-layouts  1.31 us (2%)
  between operations  0.64 us (1%)
    pallas_call x1, Pallas kernels, local(): pl.pallas_call(kernel, out_shape=(out, out), in_specs=[hbm] * 4, out_spec...  58.6 us
    unnamed x2, local copies, waits for them, and re-layouts  1.31 us

commit v1 on v0

--- a/solution.py
+++ b/solution.py
@@ -19,7 +19,7 @@
 def kernel(
     field, bins, tcol_h, topa_h, front, back,
     tcol, topa, fb, bb, hb, hs, fv, ga, gl, stage, img,
-    lsem, fsem, bsem, hsem, zsem, ysem, csem, isem, sx, sh, sz, sy, sc, si,
+    lsem, fsem, bsem, hsem, zsem, ysem, csem, isem, sx, sh, sz, sy, sc, si, ring, near,
 ):
     d = lax.axis_index("depth")
     y = lax.axis_index("tile")
@@ -35,12 +35,17 @@
     for cp in tload:
         cp.start()
     bar = pltpu.get_barrier_semaphore()
-    for p in range(1, NR):
-        pl.semaphore_signal(bar, inc=1, device_id=(z * NR + (xc + p) % NR, y), device_id_type=MESH)
+
+    def here(z_, x_, c_, y_):
+        pl.semaphore_signal(bar, inc=1, device_id=((z_ * NX + x_) * NC + c_, y_), device_id_type=MESH)
+
+    for p in range(1, NX):
+        here(z, (x + p) % NX, 0, y)
+    pl.when(c == 1)(lambda: here(z, x, 0, y))
     for p in range(1, NZ):
-        pl.semaphore_signal(bar, inc=1, device_id=((z + p) % NZ * NR + xc, y), device_id_type=MESH)
+        here((z + p) % NZ, x, 1, y)
     for p in (1, ny - 1):
-        pl.semaphore_signal(bar, inc=1, device_id=(d, (y + p) % ny), device_id_type=MESH)
+        here(z, x, 1, (y + p) % ny)
 
     @pl.when(y == 0)
     def _():
@@ -58,7 +63,17 @@
     def _():
         fb[:, 1:NT + 1, NS + 2:NS + 4, TOP:TOP + BR, :] = jnp.zeros((NZ, NT, 2, BR, 128), F32)
 
-    pl.semaphore_wait(bar, NR - 1 + NZ - 1 + 2)
+    def tell(sem, c_):
+        pl.semaphore_signal(sem, inc=1, device_id=((z * NX + x) * NC + c_, y), device_id_type=MESH)
+
+    @pl.when(c == 0)
+    def _():
+        pl.semaphore_wait(bar, NR - 1)
+        tell(ring, 1)
+
+    @pl.when(c == 1)
+    def _():
+        pl.semaphore_wait(ring, 1)
 
     def rows_of(zb, q):
         return pl.ds(pl.multiple_of((zb * NX + q // NC) * BR * NC + q % NC * BR, BR), BR)
@@ -318,9 +333,57 @@
             lax.fori_loop(0, 2 * NT, part, 0)
         return k
 
+    @pl.when(c == 1)
+    def _():
+        pl.semaphore_wait(bar, (NZ - 1 + 2) * NC)
+        tell(near, 0)
+
+    @pl.when(c == 0)
+    def _():
+        pl.semaphore_wait(near, 1)
+
     lax.fori_loop(0, NZ + 1, cells_in, 0)
 
+    def drain(m):
+        @pl.when(m >= NT)
+        def _():
+            tick_left(2 * (m - NT))
+            tick_left(2 * (m - NT) + 1)
+
+        zb = m - 2 * NT
+
+        @pl.when(jnp.logical_and(zb >= 0, zb < NZ))
+        def _():
+            @pl.when(z < NZ - 1)
+            def _():
+                z_copy(zb, True).wait_send()
+
+            @pl.when(z > 0)
+            def _():
+                z_copy(zb, False).wait_send()
+
+            @pl.when(y > 0)
+            def _():
+                y_copy(zb, False).wait_send()
+
+            @pl.when(y < ny - 1)
+            def _():
+                y_copy(zb, True).wait_send()
+
+            c_copy(zb).wait_send()
+
+        @pl.when(m == 2 * NT)
+        def _():
+            some = hb.at[pl.ds(0, NR - 1)]
+            pltpu.make_async_copy(some, some, sh.at[0]).wait()
+
+        @pl.when(m >= HALF - NT)
+        def _():
+            for i in range(3):
+                i_copy(3 * (m - HALF + NT) + i).wait_send()
+
     def bins_in(m, k):
+        drain(m)
         zb, j = bin_tile(m)
         got = bb.at[zb, :, :, pl.ds(pl.multiple_of(128 * j, 128), 128)]
         pltpu.make_async_copy(got, got, bsem.at[m]).wait()
@@ -336,40 +399,8 @@
 
     lax.fori_loop(0, HALF, bins_in, 0)
 
-    def ticks(n, k):
+    for n in range(2 * HALF - 2 * NT, 2 * HALF):
         tick_left(n)
-        return k
-
-    lax.fori_loop(0, 2 * HALF, ticks, 0)
-    def left(zb, k):
-        @pl.when(z < NZ - 1)
-        def _():
-            z_copy(zb, True).wait_send()
-
-        @pl.when(z > 0)
-        def _():
-            z_copy(zb, False).wait_send()
-
-        @pl.when(y > 0)
-        def _():
-            y_copy(zb, False).wait_send()
-
-        @pl.when(y < ny - 1)
-        def _():
-            y_copy(zb, True).wait_send()
-
-        c_copy(zb).wait_send()
-        return k
-
-    lax.fori_loop(0, NZ, left, 0)
-    some = hb.at[pl.ds(0, NR - 1)]
-    pltpu.make_async_copy(some, some, sh.at[0]).wait()
-
-    def shown(m, k):
-        i_copy(m).wait_send()
-        return k
-
-    lax.fori_loop(0, HALF - NT, shown, 0)
 
 
 def local(field, bin_ids, table_color, table_opacity):
@@ -401,6 +432,7 @@
             pltpu.VMEM((NZ, NT, 7, BR, 128), F32),
             dma((3,)), dma((NZ,)), dma((HALF,)), dma((1,)), dma((NZ, 2)), dma((NZ, 2)), dma((NZ,)), dma((NZ, NT)),
             dma((2 * HALF,)), dma((1,)), dma((NZ, 2)), dma((NZ, 2)), dma((NZ,)), dma((HALF,)),
+            pltpu.SemaphoreType.REGULAR, pltpu.SemaphoreType.REGULAR,
         ],
         compiler_params=pltpu.CompilerParams(
             collective_id=0, has_side_effects=True, vmem_limit_bytes=40 * 2**20),

time: 60.7 us -> 58.4 us (0.962)
  Pallas kernels: 58.6 us -> 56.3 us
    pallas_call x1, Pallas kernels: 58.6 us -> 56.3 us  [local(): pl.pallas_call(kernel, out_shape=(out, out), in_specs=[hbm] * 4, out_spec...]
where the time goes in v1:
time: 58.4 us; the launch traced here: 58.3 us
  Pallas kernels  56.3 us (96%)
  local copies, waits for them, and re-layouts  1.31 us (2%)
  between operations  0.64 us (1%)
    pallas_call x1, Pallas kernels, local(): pl.pallas_call(kernel, out_shape=(out, out), in_specs=[hbm] * 4, out_spec...  56.3 us
    unnamed x2, local copies, waits for them, and re-layouts  1.31 us

profile of v1, /device:TPU:1, one launch (start us, length us, event | category | flops | bytes accessed | tf_op | source)
XLA Modules:
  0.0 58.3 jit_solution(9919088518236706460)
XLA Ops:
  0.6 56.3 %shard_map.59 = (f32[4,16,512]{2,1,0:T(8,128)S(1)}, f32[4,16,512]{2,1,0:T(8,128)S(1)}) custom-call(f32[2,512,512]{2,1,0:T(8,128)} %field.1, s32[2,512,512]{2,1,0:T(8,128)} %bins.1, bf16[3,256]{1,0:T(4,128)(2,1)} %tcol_h.1, bf16[256]{0:T(256)(128)(2,1)} %topa_h.1), custom_call_target="tpu_custom_call" | custom-call | tf_op jit(solution)/shard_map/pallas_call | solution.py:416
  57.0 0.7 %copy.8 = f32[4,16,512]{2,1,0:T(8,128)} copy(f32[4,16,512]{2,1,0:T(8,128)S(1)} %get-tuple-element.4) | data formatting | bytes 262144
  57.6 0.7 %copy.9 = f32[4,16,512]{2,1,0:T(8,128)} copy(f32[4,16,512]{2,1,0:T(8,128)S(1)} %get-tuple-element.5) | data formatting | bytes 262144

commit v2 on v1

--- a/solution.py
+++ b/solution.py
@@ -308,15 +308,18 @@
         t = (ts[0] * ts[1]) * (ts[2] * ts[3])
         for n in range(3):
             acc = img[NZ - 1, j, n]
-            for s in range(NZ - 2, -1, -1):
+            for s in range(NZ - 2, 0, -1):
                 acc = img[s, j, n] + ts[s] * acc
-            front[n, :, lanes] = acc
+            front[0, n, :, lanes] = img[0, j, n]
+            front[1, n, :, lanes] = ts[0] * acc
             acc = img[0, j, 3 + n]
-            for s in range(1, NZ):
+            for s in range(1, NZ - 1):
                 acc = img[s, j, 3 + n] + ts[s] * acc
-            back[n, :, lanes] = acc
-        front[3, :, lanes] = t
-        back[3, :, lanes] = t
+            back[0, n, :, lanes] = img[NZ - 1, j, 3 + n]
+            back[1, n, :, lanes] = ts[NZ - 1] * acc
+        for part, value in ((0, jnp.zeros_like(t)), (1, t)):
+            front[part, 3, :, lanes] = value
+            back[part, 3, :, lanes] = value
 
     def cells_in(n, k):
         pl.when(n < NZ)(lambda: pass_on(n))
@@ -405,7 +408,7 @@
 
 def local(field, bin_ids, table_color, table_opacity):
     cols = field.shape[2]
-    out = jax.ShapeDtypeStruct((4, BR, cols), F32)
+    out = jax.ShapeDtypeStruct((2, 4, BR, cols), F32)
     vm = pl.BlockSpec(memory_space=pltpu.VMEM)
     hbm = pl.BlockSpec(memory_space=pltpu.HBM)
     dma = pltpu.SemaphoreType.DMA
@@ -413,7 +416,7 @@
         pltpu.with_memory_space_constraint(a, pltpu.HBM)
         for a in (field, bin_ids, table_color, table_opacity)
     ]
-    return pl.pallas_call(
+    front, back = pl.pallas_call(
         kernel,
         out_shape=(out, out),
         in_specs=[hbm] * 4,
@@ -437,6 +440,7 @@
         compiler_params=pltpu.CompilerParams(
             collective_id=0, has_side_effects=True, vmem_limit_bytes=40 * 2**20),
     )(*args)
+    return front[0] + front[1], back[0] + back[1]
 
 
 def solution(mesh):

time: 58.4 us -> 57.8 us (0.990)
  local copies, waits for them, and re-layouts: 1.31 us -> 0 us
  other arithmetic: 0 us -> 0.73 us
    unnamed x2 -> x0, local copies, waits for them, and re-layouts: 1.31 us -> none
    add x0 -> x1, other arithmetic: none -> 0.73 us  [local(): return (front[0] + front[1], back[0] + back[1])]
where the time goes in v2:
time: 57.8 us; the launch traced here: 57.7 us
  Pallas kernels  56.3 us (97%)
  other arithmetic  0.73 us (1%)
  between operations  0.64 us (1%)
    pallas_call x1, Pallas kernels, local(): pl.pallas_call(kernel, out_shape=(out, out), in_specs=[hbm] * 4, out_spec...  56.3 us

profile of v2, /device:TPU:1, one launch (start us, length us, event | category | flops | bytes accessed | tf_op | source)
XLA Modules:
  0.0 57.7 jit_solution(1300258334725901638)
XLA Ops:
  0.6 56.3 %shard_map.59 = (f32[2,4,16,512]{3,2,1,0:T(8,128)S(1)}, f32[2,4,16,512]{3,2,1,0:T(8,128)S(1)}) custom-call(f32[2,512,512]{2,1,0:T(8,128)} %field.1, s32[2,512,512]{2,1,0:T(8,128)} %bins.1, bf16[3,256]{1,0:T(4,128)(2,1)} %tcol_h.1, bf16[256]{0:T(256)(128)(2,1)} %topa_h.1), custom_call_target="tpu_custom_call" | custom-call | tf_op jit(solution)/shard_map/pallas_call | solution.py:419
  57.0 0.7 %add_bitcast_fusion = (f32[4,16,512]{2,1,0:T(8,128)}, f32[4,16,512]{2,1,0:T(8,128)}) fusion(f32[2,4,16,512]{3,2,1,0:T(8,128)S(1)} %get-tuple-element.5, f32[2,4,16,512]{3,2,1,0:T(8,128)S(1)} %get-tuple-element.4), kind=kLoop, calls=%fused_computation | loop fusion | flops 65536 | bytes 786432 | tf_op jit(solution)/shard_map/add | solution.py:443

commit v3 on v2

--- a/solution.py
+++ b/solution.py
@@ -18,8 +18,8 @@
 
 def kernel(
     field, bins, tcol_h, topa_h, front, back,
-    tcol, topa, fb, bb, hb, hs, fv, ga, gl, stage, img,
-    lsem, fsem, bsem, hsem, zsem, ysem, csem, isem, sx, sh, sz, sy, sc, si, ring, near,
+    tcol, topa, fb, bb, hb, hs, hp, ho, fv, ga, gl, stage, img,
+    lsem, fsem, bsem, hsem, zsem, ysem, csem, isem, sx, sh, sz, sy, sc, si, osem, so, ring, near,
 ):
     d = lax.axis_index("depth")
     y = lax.axis_index("tile")
@@ -125,7 +125,10 @@
 
         def one(p, k):
             q = (xc + p) % NR
-            copy_x(hs.at[q], hb.at[xc], sh.at[0], hsem.at[0], q).start()
+
+            @pl.when(q // NC != (x + 2) % NX)
+            def _():
+                copy_x(hs.at[q], hb.at[xc], sh.at[0], hsem.at[0], q).start()
             return k
 
         lax.fori_loop(1, NR, one, 0)
@@ -146,7 +149,7 @@
                         hs[q, zb // 2, j, o:o + 2, :] = jnp.zeros((2, 128), F32)
 
     send_h()
-    lax.fori_loop(NT, 2 * HALF, send_tick, 0)
+    lax.fori_loop(NT, HALF, send_tick, 0)
 
     for cp in tload:
         cp.wait()
@@ -201,15 +204,61 @@
         c_copy(zb).start()
 
     def rows_in(i, k, at):
-        for zb in range(NZ):
-            for s in range(2):
-                a = zb % 2 * 4 + s * 2
-                for j in range(NT):
-                    fb[zb, j + 1, 2 + 2 * i + s, at:at + 2, :] = hb[i, zb // 2, j, a:a + 2, :]
+        @pl.when(i // NC != (x + 2) % NX)
+        def _():
+            for zb in range(NZ):
+                for s in range(2):
+                    a = zb % 2 * 4 + s * 2
+                    for j in range(NT):
+                        fb[zb, j + 1, 2 + 2 * i + s, at:at + 2, :] = hb[i, zb // 2, j, a:a + 2, :]
         return k
 
+    to_x = x + 2 * c - 1
+
+    def o_copy(zb):
+        to_b = zb + (to_x + NX) // NX - 1
+        return pltpu.make_async_remote_copy(
+            src_ref=hp.at[zb], dst_ref=ho.at[to_b], send_sem=so.at[zb], recv_sem=osem.at[to_b],
+            device_id=((z * NX + (to_x + NX) % NX) * NC + 1 - c, y), device_id_type=MESH)
+
+    def o_goes(zb):
+        to_b = zb + (to_x + NX) // NX - 1
+        return jnp.logical_and(to_b >= 0, to_b < NZ)
+
+    def o_send(zb):
+        for core, at in ((0, TOP), (1, TOP + BR - 2)):
+            @pl.when(c == core)
+            def _():
+                for i in range(4):
+                    s = 2 + 2 * NC * ((to_x + 2 + NX) % NX) + i
+                    for j in range(NT):
+                        hp[zb, j, 2 * i:2 * i + 2, :] = fb[zb, j + 1, s, at:at + 2, :]
+
+        pl.when(o_goes(zb))(lambda: o_copy(zb).start())
+
+    def o_in(zb):
+        edge = (1 - c) * (x * NZ + zb) + c * ((NX - 1 - x) * NZ + NZ - 1 - zb) == 0
+
+        @pl.when(edge)
+        def _():
+            ho[zb] = jnp.zeros((NT, 8, 128), F32)
+
+        @pl.when(jnp.logical_not(edge))
+        def _():
+            got = ho.at[zb]
+            pltpu.make_async_copy(got, got, osem.at[zb]).wait()
+
+        for core, at in ((0, TOP - 2), (1, TOP + BR)):
+            @pl.when(c == core)
+            def _():
+                for i in range(4):
+                    s = 2 + 2 * NC * ((x + 2) % NX) + i
+                    for j in range(NT):
+                        fb[zb, j + 1, s, at:at + 2, :] = ho[zb, j, 2 * i:2 * i + 2, :]
+
     def all_rows_in():
-        pltpu.make_async_copy(hb, hb, hsem.at[0]).wait()
+        near_by = hb.at[pl.ds(0, NR - NC)]
+        pltpu.make_async_copy(near_by, near_by, hsem.at[0]).wait()
 
         @pl.when(c == 0)
         def _():
@@ -322,18 +371,29 @@
             back[part, 3, :, lanes] = value
 
     def cells_in(n, k):
-        pl.when(n < NZ)(lambda: pass_on(n))
+        pass_on(n)
+        o_send(n)
         pl.when(n == 1)(all_rows_in)
 
-        @pl.when(n > 0)
-        def _():
-            halos(n - 1)
-
-            def part(h, k2):
-                gradients(n - 1, h // 2, h % 2)
-                return k2
-
-            lax.fori_loop(0, 2 * NT, part, 0)
+        @pl.when(n == NZ - 2)
+        def _():
+            lax.fori_loop(HALF, HALF + NT, send_tick, 0)
+
+        @pl.when(n == NZ - 1)
+        def _():
+            lax.fori_loop(HALF + NT, 2 * HALF, send_tick, 0)
+
+        return k
+
+    def shape(n, k):
+        halos(n)
+        o_in(n)
+
+        def part(h, k2):
+            gradients(n, h // 2, h % 2)
+            return k2
+
+        lax.fori_loop(0, 2 * NT, part, 0)
         return k
 
     @pl.when(c == 1)
@@ -345,7 +405,8 @@
     def _():
         pl.semaphore_wait(near, 1)
 
-    lax.fori_loop(0, NZ + 1, cells_in, 0)
+    lax.fori_loop(0, NZ, cells_in, 0)
+    lax.fori_loop(0, NZ, shape, 0)
 
     def drain(m):
         @pl.when(m >= NT)
@@ -374,10 +435,11 @@
                 y_copy(zb, True).wait_send()
 
             c_copy(zb).wait_send()
+            pl.when(o_goes(zb))(lambda: o_copy(zb).wait_send())
 
         @pl.when(m == 2 * NT)
         def _():
-            some = hb.at[pl.ds(0, NR - 1)]
+            some = hb.at[pl.ds(0, NR - NC - 1)]
             pltpu.make_async_copy(some, some, sh.at[0]).wait()
 
         @pl.when(m >= HALF - NT)
@@ -428,6 +490,8 @@
             pltpu.VMEM((NZ, NS, BR, cols), jnp.int32),
             pltpu.VMEM((NR, 2, NT, 8, 128), F32),
             pltpu.VMEM((NR, 2, NT, 8, 128), F32),
+            pltpu.VMEM((NZ, NT, 8, 128), F32),
+            pltpu.VMEM((NZ, NT, 8, 128), F32),
             pltpu.VMEM(field.shape, F32),
             pltpu.VMEM((NZ, NS, BR, cols), F32),
             pltpu.VMEM((NZ, NS, BR, cols), F32),
@@ -435,7 +499,7 @@
             pltpu.VMEM((NZ, NT, 7, BR, 128), F32),
             dma((3,)), dma((NZ,)), dma((HALF,)), dma((1,)), dma((NZ, 2)), dma((NZ, 2)), dma((NZ,)), dma((NZ, NT)),
             dma((2 * HALF,)), dma((1,)), dma((NZ, 2)), dma((NZ, 2)), dma((NZ,)), dma((HALF,)),
-            pltpu.SemaphoreType.REGULAR, pltpu.SemaphoreType.REGULAR,
+            dma((NZ,)), dma((NZ,)), pltpu.SemaphoreType.REGULAR, pltpu.SemaphoreType.REGULAR,
         ],
         compiler_params=pltpu.CompilerParams(
             collective_id=0, has_side_effects=True, vmem_limit_bytes=40 * 2**20),

time: 57.8 us -> 57.2 us (0.990)
  Pallas kernels: 56.3 us -> 55.7 us
    pallas_call x1, Pallas kernels: 56.3 us -> 55.7 us  [local(): pl.pallas_call(kernel, out_shape=(out, out), in_specs=[hbm] * 4, out_spec...]
where the time goes in v3:
time: 57.2 us; the launch traced here: 57.1 us
  Pallas kernels  55.7 us (97%)
  other arithmetic  0.73 us (1%)
  between operations  0.64 us (1%)
    pallas_call x1, Pallas kernels, local(): pl.pallas_call(kernel, out_shape=(out, out), in_specs=[hbm] * 4, out_spec...  55.7 us

profile of v3, /device:TPU:1, one launch (start us, length us, event | category | flops | bytes accessed | tf_op | source)
XLA Modules:
  0.0 57.1 jit_solution(1381773311730912102)
XLA Ops:
  0.6 55.7 %shard_map.59 = (f32[2,4,16,512]{3,2,1,0:T(8,128)S(1)}, f32[2,4,16,512]{3,2,1,0:T(8,128)S(1)}) custom-call(f32[2,512,512]{2,1,0:T(8,128)} %field.1, s32[2,512,512]{2,1,0:T(8,128)} %bins.1, bf16[3,256]{1,0:T(4,128)(2,1)} %tcol_h.1, bf16[256]{0:T(256)(128)(2,1)} %topa_h.1), custom_call_target="tpu_custom_call" | custom-call | tf_op jit(solution)/shard_map/pallas_call | solution.py:481
  56.3 0.7 %add_bitcast_fusion = (f32[4,16,512]{2,1,0:T(8,128)}, f32[4,16,512]{2,1,0:T(8,128)}) fusion(f32[2,4,16,512]{3,2,1,0:T(8,128)S(1)} %get-tuple-element.5, f32[2,4,16,512]{3,2,1,0:T(8,128)S(1)} %get-tuple-element.4), kind=kLoop, calls=%fused_computation | loop fusion | flops 65536 | bytes 786432 | tf_op jit(solution)/shard_map/add | solution.py:507

commit v4 on v3

--- a/solution.py
+++ b/solution.py
@@ -110,15 +110,15 @@
                 def one(p, k2):
                     q = (xc + p) % NR
                     src, dst = tick_refs(n, q)[kind]
-                    copy_x(src, dst, sx.at[n], recv, q).start()
+                    copy_x(src, dst, sx.at[kind], recv, q).start()
                     return k2
 
                 lax.fori_loop(1, NR, one, 0)
         return k
 
-    def tick_left(n):
-        some = bb.at[0, pl.ds(0, NS - 2), :, pl.ds(0, 128)]
-        pltpu.make_async_copy(some, some, sx.at[n]).wait()
+    def ticks_left(kind):
+        some = bb.at[:, pl.ds(0, NS - 2)]
+        pltpu.make_async_copy(some, some, sx.at[kind]).wait()
 
     def send_h():
         pltpu.make_async_copy(hs.at[xc], hb.at[xc], hsem.at[0]).start()
@@ -164,21 +164,21 @@
         src = fb.at[zb, pl.ds(1, NT), pl.ds(NS if up else 2, 2), pl.ds(TOP, BR), :]
         dst = fb.at[zb, pl.ds(1, NT), pl.ds(0 if up else NS + 2, 2), pl.ds(TOP, BR), :]
         return pltpu.make_async_remote_copy(
-            src_ref=src, dst_ref=dst, send_sem=sz.at[zb, int(up)], recv_sem=zsem.at[zb, int(up)],
+            src_ref=src, dst_ref=dst, send_sem=sz.at[int(up)], recv_sem=zsem.at[zb, int(up)],
             device_id=(d + (NR if up else -NR), y), device_id_type=MESH)
 
     def y_copy(zb, right):
         src = fb.at[zb, NT if right else 1, pl.ds(2, NS), pl.ds(TOP, BR), :]
         dst = fb.at[zb, 0 if right else NT + 1, pl.ds(2, NS), pl.ds(TOP, BR), :]
         return pltpu.make_async_remote_copy(
-            src_ref=src, dst_ref=dst, send_sem=sy.at[zb, int(right)], recv_sem=ysem.at[zb, int(right)],
+            src_ref=src, dst_ref=dst, send_sem=sy.at[int(right)], recv_sem=ysem.at[zb, int(right)],
             device_id=(d, y + (1 if right else -1)), device_id_type=MESH)
 
     def c_copy(zb):
         src = fb.at[zb, pl.ds(1, NT), pl.ds(2, NS), pl.ds(pl.multiple_of(TOP + 8 * (1 - c), 8), 8), :]
         dst = fb.at[zb, pl.ds(1, NT), pl.ds(2, NS), pl.ds(pl.multiple_of((TOP + BR) * c, 8), 8), :]
         return pltpu.make_async_remote_copy(
-            src_ref=src, dst_ref=dst, send_sem=sc.at[zb], recv_sem=csem.at[zb],
+            src_ref=src, dst_ref=dst, send_sem=sc.at[0], recv_sem=csem.at[zb],
             device_id=(d + 1 - 2 * c, y), device_id_type=MESH)
 
     def pass_on(zb):
@@ -218,7 +218,7 @@
     def o_copy(zb):
         to_b = zb + (to_x + NX) // NX - 1
         return pltpu.make_async_remote_copy(
-            src_ref=hp.at[zb], dst_ref=ho.at[to_b], send_sem=so.at[zb], recv_sem=osem.at[to_b],
+            src_ref=hp.at[zb], dst_ref=ho.at[to_b], send_sem=so.at[0], recv_sem=osem.at[to_b],
             device_id=((z * NX + (to_x + NX) % NX) * NC + 1 - c, y), device_id_type=MESH)
 
     def o_goes(zb):
@@ -343,15 +343,14 @@
     def i_copy(m):
         zb, j = bin_tile(m)
         return pltpu.make_async_remote_copy(
-            src_ref=stage.at[m], dst_ref=img.at[z, j], send_sem=si.at[m], recv_sem=isem.at[z, j],
+            src_ref=stage.at[m], dst_ref=img.at[z, j], send_sem=si.at[0], recv_sem=isem.at[j],
             device_id=(zb * NR + xc, y), device_id_type=MESH)
 
     def finish(m):
         j = m % NT
         img[z, j] = stage[m]
-        for p in range(1, NZ):
-            other = img.at[(z + p) % NZ, j]
-            pltpu.make_async_copy(other, other, isem.at[(z + p) % NZ, j]).wait()
+        others = stage.at[pl.ds(0, NZ - 1)]
+        pltpu.make_async_copy(others, others, isem.at[j]).wait()
         lanes = pl.ds(pl.multiple_of(128 * j, 128), 128)
         ts = [img[s, j, 6] for s in range(NZ)]
         t = (ts[0] * ts[1]) * (ts[2] * ts[3])
@@ -408,47 +407,25 @@
     lax.fori_loop(0, NZ, cells_in, 0)
     lax.fori_loop(0, NZ, shape, 0)
 
-    def drain(m):
-        @pl.when(m >= NT)
-        def _():
-            tick_left(2 * (m - NT))
-            tick_left(2 * (m - NT) + 1)
-
-        zb = m - 2 * NT
-
-        @pl.when(jnp.logical_and(zb >= 0, zb < NZ))
-        def _():
-            @pl.when(z < NZ - 1)
-            def _():
-                z_copy(zb, True).wait_send()
-
-            @pl.when(z > 0)
-            def _():
-                z_copy(zb, False).wait_send()
-
-            @pl.when(y > 0)
-            def _():
-                y_copy(zb, False).wait_send()
-
-            @pl.when(y < ny - 1)
-            def _():
-                y_copy(zb, True).wait_send()
-
-            c_copy(zb).wait_send()
-            pl.when(o_goes(zb))(lambda: o_copy(zb).wait_send())
-
-        @pl.when(m == 2 * NT)
-        def _():
-            some = hb.at[pl.ds(0, NR - NC - 1)]
-            pltpu.make_async_copy(some, some, sh.at[0]).wait()
-
-        @pl.when(m >= HALF - NT)
-        def _():
-            for i in range(3):
-                i_copy(3 * (m - HALF + NT) + i).wait_send()
+    def wait_all(some, sem):
+        pltpu.make_async_copy(some, some, sem).wait()
+
+    def drain():
+        ticks_left(0)
+        wait_all(hb.at[pl.ds(0, NR - NC - 1)], sh.at[0])
+        planes = fb.at[:, pl.ds(1, NT), pl.ds(0, 2), pl.ds(TOP, BR), :]
+        sides = fb.at[:, 0, pl.ds(2, NS), pl.ds(TOP, BR), :]
+        pl.when(z < NZ - 1)(lambda: wait_all(planes, sz.at[1]))
+        pl.when(z > 0)(lambda: wait_all(planes, sz.at[0]))
+        pl.when(y > 0)(lambda: wait_all(sides, sy.at[0]))
+        pl.when(y < ny - 1)(lambda: wait_all(sides, sy.at[1]))
+        wait_all(fb.at[:, pl.ds(1, NT), pl.ds(2, NS), pl.ds(0, 8), :], sc.at[0])
+        around = to_x + NX != (to_x + NX) % NX + NX
+        pl.when(around)(lambda: wait_all(ho.at[pl.ds(0, NZ - 1)], so.at[0]))
+        pl.when(jnp.logical_not(around))(lambda: wait_all(ho, so.at[0]))
 
     def bins_in(m, k):
-        drain(m)
+        pl.when(m == HALF - NT)(drain)
         zb, j = bin_tile(m)
         got = bb.at[zb, :, :, pl.ds(pl.multiple_of(128 * j, 128), 128)]
         pltpu.make_async_copy(got, got, bsem.at[m]).wait()
@@ -464,8 +441,8 @@
 
     lax.fori_loop(0, HALF, bins_in, 0)
 
-    for n in range(2 * HALF - 2 * NT, 2 * HALF):
-        tick_left(n)
+    ticks_left(1)
+    wait_all(stage.at[pl.ds(0, HALF - NT)], si.at[0])
 
 
 def local(field, bin_ids, table_color, table_opacity):
@@ -497,9 +474,9 @@
             pltpu.VMEM((NZ, NS, BR, cols), F32),
             pltpu.VMEM((HALF, 7, BR, 128), F32),
             pltpu.VMEM((NZ, NT, 7, BR, 128), F32),
-            dma((3,)), dma((NZ,)), dma((HALF,)), dma((1,)), dma((NZ, 2)), dma((NZ, 2)), dma((NZ,)), dma((NZ, NT)),
-            dma((2 * HALF,)), dma((1,)), dma((NZ, 2)), dma((NZ, 2)), dma((NZ,)), dma((HALF,)),
-            dma((NZ,)), dma((NZ,)), pltpu.SemaphoreType.REGULAR, pltpu.SemaphoreType.REGULAR,
+            dma((3,)), dma((NZ,)), dma((HALF,)), dma((1,)), dma((NZ, 2)), dma((NZ, 2)), dma((NZ,)), dma((NT,)),
+            dma((2,)), dma((1,)), dma((2,)), dma((2,)), dma((1,)), dma((1,)), dma((NZ,)), dma((1,)),
+            pltpu.SemaphoreType.REGULAR, pltpu.SemaphoreType.REGULAR,
         ],
         compiler_params=pltpu.CompilerParams(
             collective_id=0, has_side_effects=True, vmem_limit_bytes=40 * 2**20),

time: 57.2 us -> 56.5 us (0.988)
  Pallas kernels: 55.7 us -> 55 us
    pallas_call x1, Pallas kernels: 55.7 us -> 55 us  [local(): pl.pallas_call(kernel, out_shape=(out, out), in_specs=[hbm] * 4, out_spec...]
where the time goes in v4:
time: 56.5 us; the launch traced here: 56.4 us
  Pallas kernels  55 us (97%)
  other arithmetic  0.73 us (1%)
  between operations  0.64 us (1%)
    pallas_call x1, Pallas kernels, local(): pl.pallas_call(kernel, out_shape=(out, out), in_specs=[hbm] * 4, out_spec...  55 us

profile of v4, /device:TPU:1, one launch (start us, length us, event | category | flops | bytes accessed | tf_op | source)
XLA Modules:
  0.0 56.4 jit_solution(5649971243692358518)
XLA Ops:
  0.6 55.0 %shard_map.59 = (f32[2,4,16,512]{3,2,1,0:T(8,128)S(1)}, f32[2,4,16,512]{3,2,1,0:T(8,128)S(1)}) custom-call(f32[2,512,512]{2,1,0:T(8,128)} %field.1, s32[2,512,512]{2,1,0:T(8,128)} %bins.1, bf16[3,256]{1,0:T(4,128)(2,1)} %tcol_h.1, bf16[256]{0:T(256)(128)(2,1)} %topa_h.1), custom_call_target="tpu_custom_call" | custom-call | tf_op jit(solution)/shard_map/pallas_call | solution.py:458
  55.7 0.7 %add_bitcast_fusion = (f32[4,16,512]{2,1,0:T(8,128)}, f32[4,16,512]{2,1,0:T(8,128)}) fusion(f32[2,4,16,512]{3,2,1,0:T(8,128)S(1)} %get-tuple-element.5, f32[2,4,16,512]{3,2,1,0:T(8,128)S(1)} %get-tuple-element.4), kind=kLoop, calls=%fused_computation | loop fusion | flops 65536 | bytes 786432 | tf_op jit(solution)/shard_map/add | solution.py:484

commit v5 on v4

--- a/solution.py
+++ b/solution.py
@@ -153,12 +153,10 @@
 
     for cp in tload:
         cp.wait()
-    tc = tcol[...].astype(F32)
-    to_ = topa[...].astype(F32).reshape(1, -1) * (1.0 / 144.0)
-    tabs = []
-    for k in range(3):
-        tabs.append([jnp.broadcast_to(tc[k:k + 1, 128 * h:128 * h + 128], (8, 128)) for h in range(2)])
-    tabs.append([jnp.broadcast_to(to_[:, 128 * h:128 * h + 128], (8, 128)) for h in range(2)])
+    tc = (tcol[...].astype(F32) * 8192.0).astype(jnp.int32)
+    to_ = (topa[...].astype(F32).reshape(1, -1) * 16384.0).astype(jnp.int32)
+    words = [tc[0:1] + tc[1:2] * 16384, tc[2:3] + to_ * 16384]
+    tabs = [[jnp.broadcast_to(w[:, 128 * h:128 * h + 128], (8, 128)) for h in range(2)] for w in words]
 
     def z_copy(zb, up):
         src = fb.at[zb, pl.ds(1, NT), pl.ds(NS if up else 2, 2), pl.ds(TOP, BR), :]
@@ -288,7 +286,7 @@
         c_copy(zb).wait_recv()
 
     lane = lax.broadcasted_iota(jnp.int32, (8, 128), 1)
-    kd, kr, kc = 0.7 * 0.48 / 12.0, 0.7 * 0.6 / 12.0, 0.7 * 0.64 / 12.0
+    kd, kr, kc = [0.7 * w / 12.0 / 8192.0 for w in (0.48, 0.6, 0.64)]
 
     def gradients(zb, j, g):
         r = pl.multiple_of(TOP + 8 * g, 8)
@@ -310,9 +308,9 @@
             gc = 8.0 * (r1 - l1) + (l2 - r2)
             q = gd * gd + gr * gr + gc * gc
             inv = lax.rsqrt(q * (1.0 / 144.0) + 1.0)
-            a = q * (inv * inv)
+            a = q * (inv * inv) * (1.0 / (144.0 * 16384.0))
             ga[zb, s, rows, lanes] = a
-            gl[zb, s, rows, lanes] = a * (0.3 + jnp.abs(kd * gd + kr * gr + kc * gc) * inv)
+            gl[zb, s, rows, lanes] = a * (0.3 / 8192.0 + jnp.abs(kd * gd + kr * gr + kc * gc) * inv)
 
     def shade(zb, j, g, m):
         rows = pl.ds(pl.multiple_of(8 * g, 8), 8)
@@ -324,12 +322,13 @@
             ids = bb[zb, s, rows, lanes]
             low = ids & 127
             upper = ids >= 128
-            look = [
+            picked = [
                 jnp.where(upper,
                           jnp.take_along_axis(hi, low, axis=1, mode="promise_in_bounds"),
                           jnp.take_along_axis(lo, low, axis=1, mode="promise_in_bounds"))
                 for lo, hi in tabs
             ]
+            look = [f(w).astype(F32) for w in picked for f in (lambda w: w & 16383, lambda w: w >> 14)]
             keep = 1.0 - look[3] * ga[zb, s, rows, lanes]
             w = look[3] * gl[zb, s, rows, lanes]
             for k in range(3):

time: 56.5 us -> 56.4 us (level)
  no operation moved by 1% of the time
where the time goes in v5:
time: 56.4 us; the launch traced here: 56.3 us
  Pallas kernels  54.9 us (97%)
  other arithmetic  0.73 us (1%)
  between operations  0.64 us (1%)
    pallas_call x1, Pallas kernels, local(): pl.pallas_call(kernel, out_shape=(out, out), in_specs=[hbm] * 4, out_spec...  54.9 us

profile of v5, /device:TPU:1, one launch (start us, length us, event | category | flops | bytes accessed | tf_op | source)
XLA Modules:
  0.0 56.3 jit_solution(16194832205421906498)
XLA Ops:
  0.6 54.9 %shard_map.59 = (f32[2,4,16,512]{3,2,1,0:T(8,128)S(1)}, f32[2,4,16,512]{3,2,1,0:T(8,128)S(1)}) custom-call(f32[2,512,512]{2,1,0:T(8,128)} %field.1, s32[2,512,512]{2,1,0:T(8,128)} %bins.1, bf16[3,256]{1,0:T(4,128)(2,1)} %tcol_h.1, bf16[256]{0:T(256)(128)(2,1)} %topa_h.1), custom_call_target="tpu_custom_call" | custom-call | tf_op jit(solution)/shard_map/pallas_call | solution.py:457
  55.5 0.7 %add_bitcast_fusion = (f32[4,16,512]{2,1,0:T(8,128)}, f32[4,16,512]{2,1,0:T(8,128)}) fusion(f32[2,4,16,512]{3,2,1,0:T(8,128)S(1)} %get-tuple-element.5, f32[2,4,16,512]{3,2,1,0:T(8,128)S(1)} %get-tuple-element.4), kind=kLoop, calls=%fused_computation | loop fusion | flops 65536 | bytes 786432 | tf_op jit(solution)/shard_map/add | solution.py:483

commit v6 on v5

--- a/solution.py
+++ b/solution.py
@@ -29,11 +29,6 @@
     x = xc // NC
     c = xc % NC
 
-    load = pltpu.make_async_copy(field, fv, lsem.at[0])
-    load.start()
-    tload = [pltpu.make_async_copy(tcol_h, tcol, lsem.at[1]), pltpu.make_async_copy(topa_h, topa, lsem.at[2])]
-    for cp in tload:
-        cp.start()
     bar = pltpu.get_barrier_semaphore()
 
     def here(z_, x_, c_, y_):
@@ -46,6 +41,12 @@
         here((z + p) % NZ, x, 1, y)
     for p in (1, ny - 1):
         here(z, x, 1, (y + p) % ny)
+
+    load = pltpu.make_async_copy(field, fv, lsem.at[0])
+    load.start()
+    tload = [pltpu.make_async_copy(tcol_h, tcol, lsem.at[1]), pltpu.make_async_copy(topa_h, topa, lsem.at[2])]
+    for cp in tload:
+        cp.start()
 
     @pl.when(y == 0)
     def _():

time: 56.4 us -> 56.4 us (level)
  no operation moved by 1% of the time
where the time goes in v6:
time: 56.4 us; the launch traced here: 56.3 us
  Pallas kernels  54.9 us (97%)
  other arithmetic  0.73 us (1%)
  between operations  0.64 us (1%)
    pallas_call x1, Pallas kernels, local(): pl.pallas_call(kernel, out_shape=(out, out), in_specs=[hbm] * 4, out_spec...  54.9 us

profile of v6, /device:TPU:1, one launch (start us, length us, event | category | flops | bytes accessed | tf_op | source)
XLA Modules:
  0.0 56.3 jit_solution(16440563510840911344)
XLA Ops:
  0.6 54.9 %shard_map.59 = (f32[2,4,16,512]{3,2,1,0:T(8,128)S(1)}, f32[2,4,16,512]{3,2,1,0:T(8,128)S(1)}) custom-call(f32[2,512,512]{2,1,0:T(8,128)} %field.1, s32[2,512,512]{2,1,0:T(8,128)} %bins.1, bf16[3,256]{1,0:T(4,128)(2,1)} %tcol_h.1, bf16[256]{0:T(256)(128)(2,1)} %topa_h.1), custom_call_target="tpu_custom_call" | custom-call | tf_op jit(solution)/shard_map/pallas_call | solution.py:458
  55.5 0.7 %add_bitcast_fusion = (f32[4,16,512]{2,1,0:T(8,128)}, f32[4,16,512]{2,1,0:T(8,128)}) fusion(f32[2,4,16,512]{3,2,1,0:T(8,128)S(1)} %get-tuple-element.5, f32[2,4,16,512]{3,2,1,0:T(8,128)S(1)} %get-tuple-element.4), kind=kLoop, calls=%fused_computation | loop fusion | flops 65536 | bytes 786432 | tf_op jit(solution)/shard_map/add | solution.py:484
